TPU v7x, 32 devices: a whole 2x2x4 slice. The times are simulated.
32 devices in a mesh: row: 8 (over z, y), col: 4 (over x, core).
Axes of the slice: x: 2, y: 2, z: 4, core: 2. Of those that a mesh axis runs over, the one named last changes fastest.
Arguments:
- features: bfloat16 [256, 128, 256], P('row', 'col'), may hold values from -6 to 6
- dw_kernel: bfloat16 [7, 7, 256], replicated, may hold values from -0.875 to 0.875
- dw_bias: float32 [256], replicated, may hold values from -4 to 4
- norm_gain: float32 [256], replicated, may hold values from 0.5 to 2
- norm_bias: float32 [256], replicated, may hold values from -3 to 3
- w_expand: bfloat16 [256, 1024], replicated, may hold values from -0.375 to 0.375
- b_expand: float32 [1024], replicated, may hold values from -3 to 3
- w_reduce: bfloat16 [1024, 256], replicated, may hold values from -0.1875 to 0.1875
- b_reduce: float32 [256], replicated, may hold values from -3 to 3
- layer_scale: float32 [256], replicated, may hold values from 0.5 to 2
- w_query: bfloat16 [256, 256], replicated, may hold values from -2 to 2
- w_keyval: bfloat16 [256, 512], replicated, may hold values from -0.375 to 0.375
- rel_bias: float32 [8, 7, 31], replicated, may hold values from -8 to 250, as said below
- w_out: bfloat16 [256, 256], replicated, may hold values from -0.75 to 0.75
Outputs:
- result: bfloat16 [256, 128, 256], P('row', 'col')
Inputs may be any that keep to these rules, and one draw needn't show every extreme that they name: `rel_bias`: relative position bias of moderate size, with possibly a few much larger entries.
All inputs are finite; a program needn't handle non-finite values.
Results may differ from a plain program's by a relative error of at most 0.014.
Values may be sent and summed in bfloat16 or wider, within the bound.
A program may use at most 64 MiB of HBM per device.

v0:
```python
import jax
import jax.numpy as jnp
from jax import lax
from jax.sharding import PartitionSpec as P

HEADS = 8


def padded_2(array, sides, width):
    for axis, dim in sides:
        devices, length = (lax.axis_size(axis), array.shape[dim])
        up = [(i, (i + 1) % devices) for i in range(devices - 1)]
        down = [(j, i) for i, j in up]
        last = lax.slice_in_dim(array, length - width, length, axis=dim)
        leading = lax.slice_in_dim(array, 0, width, axis=dim)
        before = lax.ppermute(last, axis, up)
        after = lax.ppermute(leading, axis, down)
        array = jnp.concatenate([before, array, after], axis=dim)
    return array


def block_pass(
    padded,
    features,
    dw_kernel,
    dw_bias,
    norm_gain,
    norm_bias,
    w_expand,
    b_expand,
    w_reduce,
    b_reduce,
    layer_scale,
):
    tile_rows, tile_cols, channels = features.shape
    convolved = jnp.zeros((tile_rows, tile_cols, channels), jnp.float32)
    for tap_row in range(7):
        for tap_col in range(7):
            convolved = convolved + padded[
                tap_row : tap_row + tile_rows, tap_col : tap_col + tile_cols
            ].astype(jnp.float32) * dw_kernel[tap_row, tap_col].astype(jnp.float32)
    convolved = convolved + dw_bias
    average = jnp.mean(convolved, axis=-1, keepdims=True)
    centred = convolved - average
    variance = jnp.mean(centred * centred, axis=-1, keepdims=True)
    normed = (
        (centred * lax.rsqrt(variance + 1e-06) * norm_gain + norm_bias)
        .astype(jnp.bfloat16)
        .reshape(-1, channels)
    )
    hidden = jax.nn.gelu(
        jnp.dot(normed, w_expand, preferred_element_type=jnp.float32) + b_expand, approximate=False
    ).astype(jnp.bfloat16)
    reduced = jnp.dot(hidden, w_reduce, preferred_element_type=jnp.float32) + b_reduce
    summed = features.astype(jnp.float32).reshape(-1, channels) + layer_scale * reduced
    return summed.astype(jnp.bfloat16).reshape(tile_rows, tile_cols, channels)


def shards(
    features,
    dw_kernel,
    dw_bias,
    norm_gain,
    norm_bias,
    w_expand,
    b_expand,
    w_reduce,
    b_reduce,
    layer_scale,
    w_query,
    w_keyval,
    rel_bias,
    w_out,
):
    tile_rows, tile_cols, channels = features.shape
    head_dim = channels // HEADS
    extended = padded_2(features, (("row", 0),), 3)
    padded = padded_2(extended, (("col", 1),), 3)
    block_out = block_pass(
        padded,
        features,
        dw_kernel,
        dw_bias,
        norm_gain,
        norm_bias,
        w_expand,
        b_expand,
        w_reduce,
        b_reduce,
        layer_scale,
    )
    region_side = tile_rows // 8
    local_count = region_side * region_side
    pooled = (
        block_out.astype(jnp.float32)
        .reshape(region_side, 8, region_side, 8, channels)
        .mean(axis=(1, 3))
    )
    pooled = pooled.astype(jnp.bfloat16).reshape(local_count, channels)
    queries = jnp.dot(pooled, w_query, preferred_element_type=jnp.float32).astype(jnp.bfloat16)
    keyval = jnp.dot(pooled, w_keyval, preferred_element_type=jnp.float32).astype(jnp.bfloat16)
    band_keyval = lax.all_gather(keyval, "col", axis=0, tiled=True)
    columns = lax.axis_size("col")
    position = lax.axis_index("col")
    span_cols = region_side * columns
    key_count = local_count * columns
    side_index = jnp.arange(region_side, dtype=jnp.int32)
    row_offsets = side_index[None, :] - side_index[:, None] + region_side - 1
    row_onehot = (
        row_offsets[:, :, None] == jnp.arange(2 * region_side - 1, dtype=jnp.int32)[None, None, :]
    ).astype(jnp.float32)
    row_picked = jnp.einsum("rso,hoc->hrsc", row_onehot, rel_bias, precision=lax.Precision.HIGHEST)
    query_cols = position * region_side + side_index
    span_index = jnp.arange(span_cols, dtype=jnp.int32)
    col_offsets = span_index[None, :] - query_cols[:, None] + span_cols - 1
    col_onehot = (
        col_offsets[:, :, None] == jnp.arange(2 * span_cols - 1, dtype=jnp.int32)[None, None, :]
    ).astype(jnp.float32)
    both_picked = jnp.einsum(
        "hrsc,qkc->hrqsk", row_picked, col_onehot, precision=lax.Precision.HIGHEST
    )
    both_picked = both_picked.reshape(
        HEADS, region_side, region_side, region_side, columns, region_side
    )
    bias_block = jnp.transpose(both_picked, (0, 1, 2, 4, 3, 5)).reshape(
        HEADS, local_count, key_count
    )
    query_heads = queries.reshape(local_count, HEADS, head_dim)
    key_heads = band_keyval[:, :channels].reshape(key_count, HEADS, head_dim)
    value_heads = band_keyval[:, channels:].reshape(key_count, HEADS, head_dim)
    scores = (
        jnp.einsum("qhd,khd->hqk", query_heads, key_heads, preferred_element_type=jnp.float32)
        / jnp.sqrt(jnp.float32(head_dim))
        + bias_block
    )
    attn = jax.nn.softmax(scores, axis=-1).astype(jnp.bfloat16)
    context = (
        jnp.einsum("hqk,khd->qhd", attn, value_heads, preferred_element_type=jnp.float32)
        .reshape(local_count, channels)
        .astype(jnp.bfloat16)
    )
    lifted = jnp.dot(context, w_out, preferred_element_type=jnp.float32).reshape(
        region_side, 1, region_side, 1, channels
    )
    spread = jnp.broadcast_to(lifted, (region_side, 8, region_side, 8, channels)).reshape(
        tile_rows, tile_cols, channels
    )
    return (block_out.astype(jnp.float32) + spread).astype(jnp.bfloat16)


def solution(mesh):
    return jax.shard_map(
        shards,
        mesh=mesh,
        in_specs=(
            P("row", "col", None),
            P(),
            P(),
            P(),
            P(),
            P(),
            P(),
            P(),
            P(),
            P(),
            P(),
            P(),
            P(),
            P(),
        ),
        out_specs=P("row", "col", None),
        check_vma=False,
    )
```

profile of v0, /device:TPU:17, one launch (start us, length us, event | category | flops | bytes accessed | tf_op | source)
XLA Modules:
  0.0 63.0 jit_solution(17578725768879446033)
XLA Ops:
  0.0 0.9 %fusion.106 = (bf16[3,32,256]{2,1,0:T(8,128)(2,1)S(1)}, bf16[3,32,256]{2,1,0:T(8,128)(2,1)S(1)}) fusion(bf16[32,32,256]{2,1,0:T(8,128)(2,1)} %param.14), kind=kLoop, calls=%fused_computation.266 | loop fusion | bytes 196608 | tf_op jit(solution)/shard_map/slice | solution.py:15
  0.9 3.1 %collective-permute-start = (bf16[3,32,256]{2,1,0:T(8,128)(2,1)S(1)}, bf16[3,32,256]{2,1,0:T(8,128)(2,1)S(1)}, u32[]{:S(2)}, u32[]{:S(2)}) collective-permute-start(bf16[3,32,256]{2,1,0:T(8,128)(2,1)S(1)} %get-tuple-element.13), channel_id=1, source_target_pairs={{0,4},{4,8},{8,12},{12,16},{16,20},{20,24},{24,28},{1,5},{5,9},{9,... | collective-permute-start | bytes 147464 | tf_op jit(solution)/shard_map/ppermute | solution.py:16
  4.1 3.0 %collective-permute-start.1 = (bf16[3,32,256]{2,1,0:T(8,128)(2,1)S(1)}, bf16[3,32,256]{2,1,0:T(8,128)(2,1)S(1)}, u32[]{:S(2)}, u32[]{:S(2)}) collective-permute-start(bf16[3,32,256]{2,1,0:T(8,128)(2,1)S(1)} %get-tuple-element.12), channel_id=1, source_target_pairs={{4,0},{8,4},{12,8},{16,12},{20,16},{24,20},{28,24},{5,1},{9,5},{13... | collective-permute-start | bytes 147464 | tf_op jit(solution)/shard_map/ppermute | solution.py:17
  7.1 1.6 %slice_convert_fusion.48 = (f32[1,1,256]{2,1,0:T(1,128)}, f32[1,1,256]{2,1,0:T(1,128)}, f32[1,1,256]{2,1,0:T(1,128)}, f32[1,1,256]{2,1,0:T(1,128)}, f32[1,1,256]...) fusion(bf16[7,7,256]{2,1,0:T(8,128)(2,1)} %param.15), kind=kLoop, calls=%fused_computation.231 | loop fusion | flops 4864 | bytes 29184 | tf_op jit(solution)/shard_map/mul | solution.py:39
  8.8 1.0 %fusion.63 = f32[4,4,8,31]{3,1,2,0:T(4,128)S(1)} fusion(f32[8,7,31,1]{2,0,1,3:T(8,128)} %bitcast.105, s32[4,4]{1,0:T(4,128)S(1)} %subtract_add_fusion), kind=kOutput, calls=%fused_computation.161 | convolution fusion | flops 333424 | bytes 22880 | tf_op jit(solution)/shard_map/rso,hoc->hrsc/dot_general | solution.py:112
  9.8 0.4 convolution_bitcast_fusion
  10.2 1.7 %slice_convert_fusion.47 = (f32[1,1,256]{2,1,0:T(1,128)}, f32[1,1,256]{2,1,0:T(1,128)}, f32[1,1,256]{2,1,0:T(1,128)}, f32[1,1,256]{2,1,0:T(1,128)}, f32[1,1,256]...) fusion(bf16[7,7,256]{2,1,0:T(8,128)(2,1)} %param.15), kind=kLoop, calls=%fused_computation.230 | loop fusion | flops 4864 | bytes 29184 | tf_op jit(solution)/shard_map/mul | solution.py:39
  11.9 0.2 constant_dynamic-update-slice_fusion.3
  12.2 3.1 %collective-permute-start.3 = (bf16[38,3,256]{2,1,0:T(4,128)(2,1)S(1)}, bf16[38,3,256]{2,1,0:T(4,128)(2,1)S(1)}, u32[]{:S(2)}, u32[]{:S(2)}) collective-permute-start(bf16[38,3,256]{2,1,0:T(4,128)(2,1)S(1)} %get-tuple-element.8), channel_id=1, source_target_pairs={{1,0},{2,1},{3,2},{5,4},{6,5},{7,6},{9,8},{10,9},{11,10},{13,12},{... | collective-permute-start | bytes 175112 | tf_op jit(solution)/shard_map/ppermute | solution.py:17
  15.4 3.0 %collective-permute-start.2 = (bf16[38,3,256]{2,1,0:T(4,128)(2,1)S(1)}, bf16[38,3,256]{2,1,0:T(4,128)(2,1)S(1)}, u32[]{:S(2)}, u32[]{:S(2)}) collective-permute-start(bf16[38,3,256]{2,1,0:T(4,128)(2,1)S(1)} %get-tuple-element.7), channel_id=1, source_target_pairs={{0,1},{1,2},{2,3},{4,5},{5,6},{6,7},{8,9},{9,10},{10,11},{12,13},{... | collective-permute-start | bytes 175112 | tf_op jit(solution)/shard_map/ppermute | solution.py:16
  18.4 1.5 %slice_convert_fusion.46 = (f32[1,1,256]{2,1,0:T(1,128)}, f32[1,1,256]{2,1,0:T(1,128)}, f32[1,1,256]{2,1,0:T(1,128)}, f32[1,1,256]{2,1,0:T(1,128)}, f32[1,1,256]...) fusion(bf16[7,7,256]{2,1,0:T(8,128)(2,1)} %param.15), kind=kLoop, calls=%fused_computation.229 | loop fusion | flops 2816 | bytes 16896 | tf_op jit(solution)/shard_map/mul | solution.py:39
  19.9 0.2 copy.22
  20.1 0.1 copy.23
  20.2 0.2 copy.24
  20.4 22.7 %fusion.104 = (f32[32,32]{1,0:T(8,128)S(1)}, f32[32,32,256]{2,1,0:T(8,128)S(1)}) fusion(f32[256]{0:T(256)} %param.16, f32[256]{0:T(256)} %bitcast.153, bf16[38,3,256]{2,1,0:T(4,128)(2,1)S(1)} %collective-permute-done.3, bf16[38,32,256]{2,1,0:T(8,128)(2,1)} %copy-done.2, f32[256]{0:T(256)} %bitcast.154, f32[256]{0:T(256)} %bitcast.107, f32[256]{0:T(256)} %bitcast.108, ...), kind=kLoop, calls=%fused_computation.264 | loop fusion | flops 71826432 | bytes 5513216 | tf_op jit(solution)/shard_map/reduce_sum | solution.py:43
  43.2 0.4 multiply_reduce_fusion
  43.6 0.2 copy-done.6
  43.8 0.3 add_convert_fusion.1
  44.2 0.4 copy-done.8
  44.6 9.8 %fusion.14 = f32[1024,256]{1,0:T(8,128)S(1)} fusion(bf16[1024,256]{1,0:T(8,128)(2,1)S(1)} %copy-done, bf16[1024,256]{1,0:T(8,128)(2,1)S(1)} %bitcast.102, bf16[256,1024]{1,0:T(8,128)(2,1)S(1)} %copy-done.8, f32[1024]{0:T(1024)S(1)} %copy-done.9, f32[256]{0:T(256)S(1)} %copy-done.10, f32[256]{0:T(256)S(1)} %copy-done.11, bf16[1024,256]{1,0:T(8,128)(2,1)S(1)} %bitcast.99), kind=kOutput, calls=%fused_computation.64 | convolution fusion | flops 1144520704 | bytes 3151872 | tf_op jit(solution)/shard_map/dot_general | solution.py:54
  54.6 0.8 %copy-done.3 = bf16[256,512]{1,0:T(8,128)(2,1)S(1)} copy-done((bf16[256,512]{1,0:T(8,128)(2,1)S(1)}, bf16[256,512]{1,0:T(8,128)(2,1)}, u32[]{:S(2)}) %copy-start.3) | copy-done | bytes 262168
  55.4 0.1 convolution_convert_fusion.1
  55.5 5.0 %all_gather.3 = bf16[64,512]{1,0:T(8,128)(2,1)S(1)} all-gather(bf16[16,512]{1,0:T(8,128)(2,1)S(1)} %convolution_convert_fusion.1), channel_id=1, replica_groups=mesh['row'=8,'col'=4] {'col'}, dimensions={0}, use_global_device_ids=true | all-gather | bytes 81920 | tf_op jit(solution)/shard_map/all_gather | solution.py:102
  60.5 0.1 copy.19
  60.6 0.1 copy.20
  60.8 0.1 convolution_convert_fusion.2
  61.0 0.1 fusion.17
  61.2 0.2 fusion.108
  61.4 0.3 fusion.18
  61.8 0.1 fusion.59
  61.9 0.1 broadcast_in_dim.2
  62.1 1.0 %add_convert_fusion = bf16[32,32,256]{2,1,0:T(8,128)(2,1)} fusion(f32[32,32,256]{2,1,0:T(8,128)S(1)} %bitcast.97, f32[32,32,256]{2,1,0:T(8,128)S(1)} %bitcast.98), kind=kLoop, calls=%fused_computation.74 | loop fusion | flops 524288 | bytes 2621440 | tf_op jit(solution)/shard_map/convert_element_type | solution.py:148
  (40 shorter events, 0.6 us)
Async XLA Ops:
  0.0 44.2 %copy-start = (bf16[1024,256]{1,0:T(8,128)(2,1)S(1)}, bf16[1024,256]{1,0:T(8,128)(2,1)}, u32[]{:S(2)}) copy-start(bf16[1024,256]{1,0:T(8,128)(2,1)} %param.21) | copy-start | bytes 1572868
  0.0 11.9 %copy-start.1 = (bf16[32,32,256]{2,1,0:T(8,128)(2,1)S(1)}, bf16[32,32,256]{2,1,0:T(8,128)(2,1)}, u32[]{:S(2)}) copy-start(bf16[32,32,256]{2,1,0:T(8,128)(2,1)} %param.14) | copy-start | bytes 1572868
  0.9 10.9 %collective-permute-start = (bf16[3,32,256]{2,1,0:T(8,128)(2,1)S(1)}, bf16[3,32,256]{2,1,0:T(8,128)(2,1)S(1)}, u32[]{:S(2)}, u32[]{:S(2)}) collective-permute-start(bf16[3,32,256]{2,1,0:T(8,128)(2,1)S(1)} %get-tuple-element.13), channel_id=1, source_target_pairs={{0,4},{4,8},{8,12},{12,16},{16,20},{20,24},{24,28},{1,5},{5,9},{9,... | collective-permute-start | bytes 147464 | tf_op jit(solution)/shard_map/ppermute | solution.py:16
  4.1 8.0 %collective-permute-start.1 = (bf16[3,32,256]{2,1,0:T(8,128)(2,1)S(1)}, bf16[3,32,256]{2,1,0:T(8,128)(2,1)S(1)}, u32[]{:S(2)}, u32[]{:S(2)}) collective-permute-start(bf16[3,32,256]{2,1,0:T(8,128)(2,1)S(1)} %get-tuple-element.12), channel_id=1, source_target_pairs={{4,0},{8,4},{12,8},{16,12},{20,16},{24,20},{28,24},{5,1},{9,5},{13... | collective-permute-start | bytes 147464 | tf_op jit(solution)/shard_map/ppermute | solution.py:17
  12.1 6.3 %copy-start.2 = (bf16[38,32,256]{2,1,0:T(8,128)(2,1)}, bf16[38,32,256]{2,1,0:T(8,128)(2,1)S(1)}, u32[]{:S(2)}) copy-start(bf16[38,32,256]{2,1,0:T(8,128)(2,1)S(1)} %get-tuple-element.19) | copy-start | bytes 1867780
  12.2 8.2 %collective-permute-start.3 = (bf16[38,3,256]{2,1,0:T(4,128)(2,1)S(1)}, bf16[38,3,256]{2,1,0:T(4,128)(2,1)S(1)}, u32[]{:S(2)}, u32[]{:S(2)}) collective-permute-start(bf16[38,3,256]{2,1,0:T(4,128)(2,1)S(1)} %get-tuple-element.8), channel_id=1, source_target_pairs={{1,0},{2,1},{3,2},{5,4},{6,5},{7,6},{9,8},{10,9},{11,10},{13,12},{... | collective-permute-start | bytes 175112 | tf_op jit(solution)/shard_map/ppermute | solution.py:17
  15.4 5.1 %collective-permute-start.2 = (bf16[38,3,256]{2,1,0:T(4,128)(2,1)S(1)}, bf16[38,3,256]{2,1,0:T(4,128)(2,1)S(1)}, u32[]{:S(2)}, u32[]{:S(2)}) collective-permute-start(bf16[38,3,256]{2,1,0:T(4,128)(2,1)S(1)} %get-tuple-element.7), channel_id=1, source_target_pairs={{0,1},{1,2},{2,3},{4,5},{5,6},{6,7},{8,9},{9,10},{10,11},{12,13},{... | collective-permute-start | bytes 175112 | tf_op jit(solution)/shard_map/ppermute | solution.py:16
  43.1 0.7 %copy-start.6 = (f32[256]{0:T(256)S(1)}, f32[256]{0:T(256)}, u32[]{:S(2)}) copy-start(f32[256]{0:T(256)} %param.18) | copy-start | bytes 3076
  43.1 0.7 %copy-start.7 = (f32[256]{0:T(256)S(1)}, f32[256]{0:T(256)}, u32[]{:S(2)}) copy-start(f32[256]{0:T(256)} %param.17) | copy-start | bytes 3076
  43.5 1.0 %copy-start.8 = (bf16[256,1024]{1,0:T(8,128)(2,1)S(1)}, bf16[256,1024]{1,0:T(8,128)(2,1)}, u32[]{:S(2)}) copy-start(bf16[256,1024]{1,0:T(8,128)(2,1)} %param.19) | copy-start | bytes 1572868
  43.5 1.0 %copy-start.9 = (f32[1024]{0:T(1024)S(1)}, f32[1024]{0:T(1024)}, u32[]{:S(2)}) copy-start(f32[1024]{0:T(1024)} %param.20) | copy-start | bytes 12292
  43.6 1.0 %copy-start.10 = (f32[256]{0:T(256)S(1)}, f32[256]{0:T(256)}, u32[]{:S(2)}) copy-start(f32[256]{0:T(256)} %param.22) | copy-start | bytes 3076
  43.6 1.0 %copy-start.11 = (f32[256]{0:T(256)S(1)}, f32[256]{0:T(256)}, u32[]{:S(2)}) copy-start(f32[256]{0:T(256)} %param.23) | copy-start | bytes 3076
  54.4 1.0 %copy-start.3 = (bf16[256,512]{1,0:T(8,128)(2,1)S(1)}, bf16[256,512]{1,0:T(8,128)(2,1)}, u32[]{:S(2)}) copy-start(bf16[256,512]{1,0:T(8,128)(2,1)} %param.25) | copy-start | bytes 786436
  54.4 6.3 %copy-start.4 = (bf16[256,256]{1,0:T(8,128)(2,1)S(1)}, bf16[256,256]{1,0:T(8,128)(2,1)}, u32[]{:S(2)}) copy-start(bf16[256,256]{1,0:T(8,128)(2,1)} %param.24) | copy-start | bytes 393220
  54.5 7.2 %copy-start.5 = (bf16[256,256]{1,0:T(8,128)(2,1)S(1)}, bf16[256,256]{1,0:T(8,128)(2,1)}, u32[]{:S(2)}) copy-start(bf16[256,256]{1,0:T(8,128)(2,1)} %param.27) | copy-start | bytes 393220
where the time goes:
time: 64 us; the launch traced here: 63 us
  other arithmetic  29.5 us (46%)
  starting transfers between devices  12.3 us (19%)
  matrix products  12 us (19%)
  blocking collectives  5.01 us (8%)
  local copies, waits for them, and re-layouts  3.77 us (6%)
    reduce_sum x1, other arithmetic, block_pass(): average = jnp.mean(convolved, axis=-1, keepdims=True)  22.7 us
    dot_general x1, matrix products, block_pass(): jnp.dot(hidden, w_reduce, preferred_element_type=jnp.float32) + b_reduce  9.83 us
    ppermute x2, starting transfers between devices, padded_2(): after = lax.ppermute(leading, axis, down)  6.18 us
    ppermute x2, starting transfers between devices, padded_2(): before = lax.ppermute(last, axis, up)  6.15 us
    all_gather x1, blocking collectives, shards(): band_keyval = lax.all_gather(keyval, 'col', axis=0, tiled=True)  5.01 us
    mul x3, other arithmetic, block_pass(): padded[tap_row:tap_row + tile_rows, tap_col:tap_col + tile_cols]  4.8 us
    unnamed x25, local copies, waits for them, and re-layouts  1.48 us
  transfers between devices with their start and end apart: 4, of which 0 were waited for; matrix products, arithmetic and copies ran while one was open for 11% of the time, Pallas kernels for 0%

commit v1 on v0

v1 whole, which is shorter than its diff:
```python
import functools

import jax
import jax.numpy as jnp
from jax import lax
from jax.experimental import pallas as pl
from jax.experimental.pallas import tpu as pltpu
from jax.sharding import PartitionSpec as P

HEADS = 8
T = 32
W = 48
L = 8
MESH = pl.DeviceIdType.MESH
F32 = jnp.float32
BF16 = jnp.bfloat16


def dot(a, b):
    return jnp.dot(a, b, preferred_element_type=F32)


def gelu(x):
    return (0.5 * x) * (1.0 + lax.erf(x * 0.7071067811865476))


def kernel(
    n_row,
    n_col,
    feat,
    dw,
    dw_bias,
    gain,
    nbias,
    we_hbm,
    b_exp,
    wr_hbm,
    b_red,
    scale,
    wq_hbm,
    wkv_hbm,
    table,
    wo_hbm,
    out,
    we,
    wr,
    wq,
    wkv,
    wo,
    xs,
    taps,
    wb,
    norm,
    block,
    psum,
    bias,
    stage,
    rowbuf,
    colbuf,
    corner,
    gath,
    wsem,
    send_sem,
    recv_sem,
    gsend,
    grecv,
):
    row = lax.axis_index("row")
    col = lax.axis_index("col")
    span = 4 * n_col
    stride = 2 * span
    keys = 4 * stride

    weights = [
        pltpu.make_async_copy(s, d, wsem.at[k])
        for k, (s, d) in enumerate(
            ((we_hbm, we), (wr_hbm, wr), (wq_hbm, wq), (wkv_hbm, wkv), (wo_hbm, wo))
        )
    ]
    for c in weights:
        c.start()

    up, down = row > 0, row < n_row - 1
    left, right = col > 0, col < n_col - 1
    both = jnp.logical_and
    near = (
        (up, -1, 0),
        (down, 1, 0),
        (left, 0, -1),
        (right, 0, 1),
        (both(up, left), -1, -1),
        (both(up, right), -1, 1),
        (both(down, left), 1, -1),
        (both(down, right), 1, 1),
    )
    barrier = pltpu.get_barrier_semaphore()
    for cond, dr, dc in near:
        if dr != 0:

            @pl.when(cond)
            def _(dr=dr, dc=dc):
                pl.semaphore_signal(
                    barrier, inc=1, device_id=(row + dr, col + dc), device_id_type=MESH
                )

    for d in range(1, n_col):
        pl.semaphore_signal(
            barrier, inc=1, device_id=(row, lax.rem(col + d, n_col)), device_id_type=MESH
        )

    for h in range(2):
        lanes = slice(h * 128, h * 128 + 128)
        xs[h, 0 : 3 * W] = jnp.zeros((3 * W, 128), F32)
        xs[h, 35 * W : 38 * W] = jnp.zeros((3 * W, 128), F32)

    def widen(r, carry):
        base = pl.multiple_of((r + 3) * W, 16)
        v = feat[r].astype(F32)
        zero = jnp.zeros((8, 128), F32)
        for h in range(2):
            xs[h, pl.ds(base, 8)] = zero
            xs[h, pl.ds(base + L, T)] = v[:, h * 128 : h * 128 + 128]
            xs[h, pl.ds(base + L + T, 8)] = zero
        return carry

    lax.fori_loop(0, T, widen, 0)
    for side, first in ((0, 0), (1, T - 3)):
        for c in range(3):
            for h in range(2):
                stage[side, c, :, h * 128 : h * 128 + 128] = xs[
                    h, pl.ds(3 * W + L + first + c, T, stride=W)
                ].astype(BF16)

    number = lambda c: c.astype(jnp.int32)
    across = 1 + number(left) + number(right)
    pl.semaphore_wait(barrier, n_col - 1 + across * (number(up) + number(down)))

    def remote(src, dst, k, dr, dc):
        return pltpu.make_async_remote_copy(
            src_ref=src,
            dst_ref=dst,
            send_sem=send_sem.at[k],
            recv_sem=recv_sem.at[k],
            device_id=(row + dr, col + dc),
            device_id_type=MESH,
        )

    plan = (
        (feat.at[0:3], rowbuf.at[1]),
        (feat.at[T - 3 : T], rowbuf.at[0]),
        (stage.at[0], colbuf.at[1]),
        (stage.at[1], colbuf.at[0]),
        (stage.at[0, :, 0:16], corner.at[3]),
        (stage.at[1, :, 0:16], corner.at[2]),
        (stage.at[0, :, 16:32], corner.at[1]),
        (stage.at[1, :, 16:32], corner.at[0]),
    )
    opposite = (1, 0, 3, 2, 7, 6, 5, 4)
    sends = [remote(s, d, k, near[k][1], near[k][2]) for k, (s, d) in enumerate(plan)]
    for k, c in enumerate(sends):

        @pl.when(near[k][0])
        def _(c=c):
            c.start()

    for a in range(7):
        v = dw[a].astype(F32)
        for b in range(7):
            for h in range(2):
                wb[h, a * 7 + b] = jnp.broadcast_to(
                    v[b : b + 1, h * 128 : h * 128 + 128], (8, 128)
                )
    lane = lax.broadcasted_iota(jnp.int32, (8, keys), 1)
    valid = lax.rem(lane, stride) < span
    for r in range(4):
        t = table[r]
        for c in range(4):
            shift = keys - (span - 1) + 4 * col + c
            moved = pltpu.roll(t, shift, 1)
            bias[r * 4 + c] = jnp.where(valid, moved, -1e30)

    def halo(k):
        return sends[opposite[k]].wait_recv

    for k in range(2):

        @pl.when(near[k][0])
        def _(k=k):
            halo(k)()
            for q in range(3):
                v = rowbuf[k, q].astype(F32)
                r = q if k == 0 else T + 3 + q
                for h in range(2):
                    xs[h, r * W + L : r * W + L + T] = v[:, h * 128 : h * 128 + 128]

    for k in range(2):

        @pl.when(near[2 + k][0])
        def _(k=k):
            halo(2 + k)()
            for c in range(3):
                v = colbuf[k, c].astype(F32)
                first = 3 * W + (L - 3 if k == 0 else L + T) + c
                for h in range(2):
                    xs[h, pl.ds(first, T, stride=W)] = v[:, h * 128 : h * 128 + 128]

    for k in range(4):

        @pl.when(near[4 + k][0])
        def _(k=k):
            halo(4 + k)()
            low, far = k >= 2, k % 2 == 1
            for c in range(3):
                v = corner[k, c].astype(F32)
                for q in range(3):
                    at = (T + 3 + q if low else q) * W + (L + T if far else L - 3) + c
                    s = q if low else 13 + q
                    for h in range(2):
                        xs[h, at : at + 1] = v[s : s + 1, h * 128 : h * 128 + 128]

    def spread_rows(r, carry):
        for h in range(2):
            for m in range(10):
                taps[h, m, r] = xs[h, pl.ds(r * W + (L - 3) + m, 8, stride=4)]
        return carry

    lax.fori_loop(0, T + 6, spread_rows, 0)

    weights[0].wait()
    weights[1].wait()

    def region_row(i, carry):
        def column(j, carry):
            x = []
            for h in range(2):
                acc = jnp.broadcast_to(
                    dw_bias[:, h * 128 : h * 128 + 128].reshape(1, 1, 128), (8, 8, 128)
                )
                for b in range(7):
                    slab = taps[h, j + b, pl.ds(i * 8, 14)]
                    for a in range(7):
                        acc = acc + slab[a : a + 8] * wb[h, a * 7 + b]
                x.append(acc.reshape(64, 128))
            mean = (
                jnp.sum(x[0] + x[1], axis=-1, keepdims=True) * (1.0 / 256.0)
            )
            x = [v - mean for v in x]
            var = jnp.sum(x[0] * x[0] + x[1] * x[1], axis=-1, keepdims=True) * (1.0 / 256.0)
            inv = lax.rsqrt(var + 1e-06)
            for h in range(2):
                lanes = slice(h * 128, h * 128 + 128)
                norm[pl.ds(pl.multiple_of(j * 64, 64), 64), lanes] = (
                    x[h] * inv * gain[:, lanes] + nbias[:, lanes]
                ).astype(BF16)
            return carry

        lax.fori_loop(0, 4, column, 0)
        n = norm[...]
        red = jnp.zeros((256, 256), F32)
        for f in range(4):
            part = slice(f * 256, f * 256 + 256)
            hid = gelu(dot(n, we[:, part]) + b_exp[:, part]).astype(BF16)
            red = red + dot(hid, wr[part, :])
        red = scale[...] * (red + b_red[...])
        for h in range(2):
            total = jnp.zeros((8, 128), F32)
            for j in range(4):
                v = red[j * 64 : j * 64 + 64, h * 128 : h * 128 + 128].reshape(8, 8, 128)
                v = (v + taps[h, j + 3, pl.ds(i * 8 + 3, 8)]).astype(BF16).astype(F32)
                total = total + jnp.sum(v, axis=0)
                for r in range(8):
                    block[h, pl.ds((i * 8 + r) * T + j, 8, stride=4)] = v[r]
            psum[h, pl.ds(pl.multiple_of(i * 8, 8), 8)] = total
        return carry

    lax.fori_loop(0, 4, region_row, 0)

    pooled = jnp.concatenate(
        [
            (psum[h, pl.ds(0, 16, stride=2)] + psum[h, pl.ds(1, 16, stride=2)]) * (1.0 / 64.0)
            for h in range(2)
        ],
        axis=1,
    ).astype(BF16)
    gath[col] = pooled
    gathers = []
    for d in range(1, n_col):
        c = pltpu.make_async_remote_copy(
            src_ref=gath.at[col],
            dst_ref=gath.at[col],
            send_sem=gsend.at[d - 1],
            recv_sem=grecv.at[d - 1],
            device_id=(row, lax.rem(col + d, n_col)),
            device_id_type=MESH,
        )
        c.start()
        gathers.append(c)
    weights[2].wait()
    weights[3].wait()
    weights[4].wait()
    queries = dot(pooled, wq[...]).astype(BF16).astype(F32)
    channel = lax.broadcasted_iota(jnp.int32, (8, 256), 1)
    head = lax.broadcasted_iota(jnp.int32, (8, 256), 0)
    own = ((channel >= head * 32) & (channel < head * 32 + 32)).astype(F32)
    spread = (queries[:, None, :] * own[None]).reshape(128, 256).astype(BF16)
    key = lax.broadcasted_iota(jnp.int32, (keys, 16 * n_col), 0)
    token = lax.broadcasted_iota(jnp.int32, (keys, 16 * n_col), 1)
    place = ((token % 16) // 4) * stride + (token // 16) * 4 + token % 4
    pick = (key == place).astype(F32).astype(BF16)
    for k, c in enumerate(sends):

        @pl.when(near[k][0])
        def _(c=c):
            c.wait_send()

    for c in gathers:
        c.wait()
    tokens = gath[...].reshape(16 * n_col, 256)
    ordered = dot(pick, tokens).astype(BF16)
    keyval = dot(ordered, wkv[...]).astype(BF16)
    scores = lax.dot_general(
        spread, keyval[:, :256], (((1,), (1,)), ((), ())), preferred_element_type=F32
    )
    scores = scores * (1.0 / 32.0**0.5) + bias[...].reshape(128, keys)
    top = jnp.max(scores, axis=-1, keepdims=True)
    e = jnp.exp(scores - top)
    attn = (e / jnp.sum(e, axis=-1, keepdims=True)).astype(BF16)
    ctx = dot(attn, keyval[:, 256:]).reshape(16, 8, 256)
    ctx = jnp.sum(ctx * own[None], axis=1).astype(BF16)
    psum_lift = dot(ctx, wo[...])
    for g in range(16):
        norm_row = psum_lift[g : g + 1]
        wb[0, g] = jnp.broadcast_to(norm_row[:, :128], (8, 128))
        wb[1, g] = jnp.broadcast_to(norm_row[:, 128:], (8, 128))

    def finish(r, carry):
        i = r // 8
        parts = []
        for h in range(2):
            v = block[h, pl.ds(pl.multiple_of(r * T, T), T)].reshape(4, 8, 128)
            parts.append((v + wb[h, pl.ds(i * 4, 4)]).reshape(T, 128))
        out[r] = jnp.concatenate(parts, axis=1).astype(BF16)
        return carry

    lax.fori_loop(0, T, finish, 0)


def shards(
    n_row,
    n_col,
    features,
    dw_kernel,
    dw_bias,
    norm_gain,
    norm_bias,
    w_expand,
    b_expand,
    w_reduce,
    b_reduce,
    layer_scale,
    w_query,
    w_keyval,
    rel_bias,
    w_out,
):
    stride = 8 * n_col
    keys = 4 * stride
    padded = jnp.pad(rel_bias, ((0, 0), (0, 0), (0, 1)))
    table = jnp.stack([padded[:, 3 - r : 7 - r].reshape(HEADS, keys) for r in range(4)])
    vmem = pl.BlockSpec(memory_space=pltpu.VMEM)
    hbm = pl.BlockSpec(memory_space=pl.ANY)
    lane = lambda v: v.reshape(1, -1)
    return pl.pallas_call(
        functools.partial(kernel, n_row, n_col),
        out_shape=jax.ShapeDtypeStruct(features.shape, BF16),
        in_specs=[vmem] * 5 + [hbm, vmem, hbm, vmem, vmem, hbm, hbm, vmem, hbm],
        out_specs=vmem,
        scratch_shapes=[
            pltpu.VMEM(w_expand.shape, BF16),
            pltpu.VMEM(w_reduce.shape, BF16),
            pltpu.VMEM(w_query.shape, BF16),
            pltpu.VMEM(w_keyval.shape, BF16),
            pltpu.VMEM(w_out.shape, BF16),
            pltpu.VMEM((2, (T + 6) * W, 128), F32),
            pltpu.VMEM((2, 10, T + 6, 8, 128), F32),
            pltpu.VMEM((2, 49, 8, 128), F32),
            pltpu.VMEM((256, 256), BF16),
            pltpu.VMEM((2, T * T, 128), F32),
            pltpu.VMEM((2, 32, 128), F32),
            pltpu.VMEM((16, 8, keys), F32),
            pltpu.VMEM((2, 3, T, 256), BF16),
            pltpu.VMEM((2, 3, T, 256), BF16),
            pltpu.VMEM((2, 3, T, 256), BF16),
            pltpu.VMEM((4, 3, 16, 256), BF16),
            pltpu.VMEM((n_col, 16, 256), BF16),
            pltpu.SemaphoreType.DMA((5,)),
            pltpu.SemaphoreType.DMA((8,)),
            pltpu.SemaphoreType.DMA((8,)),
            pltpu.SemaphoreType.DMA((n_col - 1,)),
            pltpu.SemaphoreType.DMA((n_col - 1,)),
        ],
        compiler_params=pltpu.CompilerParams(
            collective_id=0, has_side_effects=True, vmem_limit_bytes=40 * 1024 * 1024
        ),
    )(
        features,
        dw_kernel,
        lane(dw_bias),
        lane(norm_gain),
        lane(norm_bias),
        w_expand,
        lane(b_expand),
        w_reduce,
        lane(b_reduce),
        lane(layer_scale),
        w_query,
        w_keyval,
        table,
        w_out,
    )


def solution(mesh):
    return jax.shard_map(
        functools.partial(shards, mesh.shape["row"], mesh.shape["col"]),
        mesh=mesh,
        in_specs=(P("row", "col", None),) + (P(),) * 13,
        out_specs=P("row", "col", None),
        check_vma=False,
    )
```

time: 64 us -> 31.7 us (0.50)
  other arithmetic: 29.5 us -> 0.01 us
  Pallas kernels: 0 us -> 23.5 us
  starting transfers between devices: 12.3 us -> 0 us
  matrix products: 12 us -> 0 us
  blocking collectives: 5.01 us -> 0 us
  local copies, waits for them, and re-layouts: 3.77 us -> 7.66 us
    pallas_call x0 -> x1, Pallas kernels: none -> 23.5 us  [shards(): pl.pallas_call(functools.partial(kernel, n_row, n_col), out_shape=jax.Sha...]
    reduce_sum x3 -> x0, other arithmetic: 23.1 us -> none  [the longest x1 22.7 us: block_pass(): average = jnp.mean(convolved, axis=-1, keepdims=True)]
    ppermute x4 -> x0, starting transfers between devices: 12.3 us -> none  [the longest x2 6.18 us: padded_2(): after = lax.ppermute(leading, axis, down)]
    dot_general x8 -> x0, matrix products: 12 us -> none  [the longest x1 9.83 us: block_pass(): jnp.dot(hidden, w_reduce, preferred_element_type=jnp.float32) + b_reduce]
    all_gather x1 -> x0, blocking collectives: 5.01 us -> none  [shards(): band_keyval = lax.all_gather(keyval, 'col', axis=0, tiled=True)]
    unnamed x25 -> x27, local copies, waits for them, and re-layouts: 1.48 us -> 6.44 us
    mul x3 -> x0, other arithmetic: 4.8 us -> none  [block_pass(): padded[tap_row:tap_row + tile_rows, tap_col:tap_col + tile_cols]]
    convert_element_type x3 -> x0, other arithmetic: 1.3 us -> none  [the longest x1 0.96 us: shards(): return (block_out.astype(jnp.float32) + spread).astype(jnp.bfloat16)]
  transfers between devices with their start and end apart: 4 -> 0, of which waited for: 0 -> 0; matrix products, arithmetic and copies ran while one was open for 11% -> 0% of each run, Pallas kernels for 0% -> 0%
where the time goes in v1:
time: 31.7 us; the launch traced here: 31.3 us
  Pallas kernels  23.5 us (74%)
  local copies, waits for them, and re-layouts  7.66 us (24%)
    pallas_call x1, Pallas kernels, shards(): pl.pallas_call(functools.partial(kernel, n_row, n_col), out_shape=jax.Sha...  23.5 us
    unnamed x27, local copies, waits for them, and re-layouts  6.44 us
    slice x5, local copies, waits for them, and re-layouts, shards(): padded[:, 3 - r:7 - r].reshape(HEADS, keys)  0.89 us

profile of v1, /device:TPU:17, one launch (start us, length us, event | category | flops | bytes accessed | tf_op | source)
XLA Modules:
  0.0 31.3 jit_solution(6263799477581803646)
XLA Ops:
  0.0 0.0 copy-start.3
  0.0 0.9 %pad_slice_fusion.3 = (f32[8,4,32]{2,0,1:T(8,128)S(1)}, f32[8,4,32]{2,0,1:T(8,128)S(1)}, f32[8,4,32]{2,0,1:T(8,128)S(1)}, f32[8,4,32]{2,0,1:T(8,128)S(1)}) fusion(f32[8,7,31]{2,0,1:T(8,128)} %param.26), kind=kLoop, calls=%fused_computation.3 | loop fusion | bytes 23328 | tf_op jit(solution)/shard_map/slice | solution.py:369
  0.9 0.1 stack_reshape.12
  1.0 0.1 stack_reshape.13
  1.1 0.1 stack_reshape.14
  1.1 0.0 copy-start.6
  1.2 0.1 stack_reshape.15
  1.2 0.0 copy-start.7
  1.2 0.0 copy-start.9
  1.2 0.0 copy-start.10
  1.2 0.0 copy-start.11
  1.3 0.0 copy-start.12
  1.3 0.0 copy-done.3
  1.3 0.6 %copy-done.6 = bf16[7,7,256]{2,1,0:T(8,128)(2,1)S(1)} copy-done((bf16[7,7,256]{2,1,0:T(8,128)(2,1)S(1)}, bf16[7,7,256]{2,1,0:T(8,128)(2,1)}, u32[]{:S(2)}) %copy-start.6) | copy-done | bytes 25112
  1.9 0.0 copy-done.7
  1.9 0.0 copy-done.8
  1.9 0.0 copy-done.9
  2.0 0.0 copy-done.10
  2.0 0.0 copy-done.11
  2.0 0.0 copy-done.12
  2.0 0.0 copy-start
  2.0 1.0 %copy-done = bf16[32,32,256]{2,1,0:T(8,128)(2,1)S(1)} copy-done((bf16[32,32,256]{2,1,0:T(8,128)(2,1)S(1)}, bf16[32,32,256]{2,1,0:T(8,128)(2,1)}, u32[]{:S(2)}) %copy-start) | copy-done | bytes 524312
  3.0 0.0 copy-start.1
  3.0 1.0 %copy-done.1 = bf16[256,1024]{1,0:T(8,128)(2,1)S(1)} copy-done((bf16[256,1024]{1,0:T(8,128)(2,1)S(1)}, bf16[256,1024]{1,0:T(8,128)(2,1)}, u32[]{:S(2)}) %copy-start.1) | copy-done | bytes 524312
  4.1 0.0 copy-start.2
  4.1 1.0 %copy-done.2 = bf16[1024,256]{1,0:T(8,128)(2,1)S(1)} copy-done((bf16[1024,256]{1,0:T(8,128)(2,1)S(1)}, bf16[1024,256]{1,0:T(8,128)(2,1)}, u32[]{:S(2)}) %copy-start.2) | copy-done | bytes 524312
  5.1 0.0 copy-start.4
  5.1 0.9 %copy-done.4 = bf16[256,256]{1,0:T(8,128)(2,1)S(1)} copy-done((bf16[256,256]{1,0:T(8,128)(2,1)S(1)}, bf16[256,256]{1,0:T(8,128)(2,1)}, u32[]{:S(2)}) %copy-start.4) | copy-done | bytes 131096
  6.0 0.0 copy-start.5
  6.0 0.9 %copy-done.5 = bf16[256,256]{1,0:T(8,128)(2,1)S(1)} copy-done((bf16[256,256]{1,0:T(8,128)(2,1)S(1)}, bf16[256,256]{1,0:T(8,128)(2,1)}, u32[]{:S(2)}) %copy-start.5) | copy-done | bytes 131096
  6.9 23.5 %shard_map.136 = bf16[32,32,256]{2,1,0:T(8,128)(2,1)S(1)} custom-call(bf16[32,32,256]{2,1,0:T(8,128)(2,1)S(1)} %copy-done, bf16[7,7,256]{2,1,0:T(8,128)(2,1)S(1)} %copy-done.6, f32[1,256]{1,0:T(1,128)S(1)} %bitcast.7, f32[1,256]{1,0:T(1,128)S(1)} %bitcast.8, f32[1,256]{1,0:T(1,128)S(1)} %bitcast.9, bf16[256,1024]{1,0:T(8,128)(2,1)S(1)} %copy-done.1, ...), custom_call_target="tpu_custom_call" | custom-call | tf_op jit(solution)/shard_map/pallas_call | solution.py:373
  30.5 0.8 %copy.20 = bf16[32,32,256]{2,1,0:T(8,128)(2,1)} copy(bf16[32,32,256]{2,1,0:T(8,128)(2,1)S(1)} %shard_map.136) | data formatting | bytes 1048576
  (6 shorter events, 0.0 us)
Async XLA Ops:
  0.0 1.3 %copy-start.3 = (bf16[256,512]{1,0:T(8,128)(2,1)S(1)}, bf16[256,512]{1,0:T(8,128)(2,1)}, u32[]{:S(2)}) copy-start(bf16[256,512]{1,0:T(8,128)(2,1)} %wkv_hbm.1) | copy-start | bytes 786436
  1.1 0.8 %copy-start.6 = (bf16[7,7,256]{2,1,0:T(8,128)(2,1)S(1)}, bf16[7,7,256]{2,1,0:T(8,128)(2,1)}, u32[]{:S(2)}) copy-start(bf16[7,7,256]{2,1,0:T(8,128)(2,1)} %dw.1) | copy-start | bytes 75268
  1.2 0.7 %copy-start.7 = (f32[1024]{0:T(1024)S(1)}, f32[1024]{0:T(1024)}, u32[]{:S(2)}) copy-start(f32[1024]{0:T(1024)} %param.20) | copy-start | bytes 12292
  1.2 0.7 %copy-start.8 = (f32[256]{0:T(256)S(1)}, f32[256]{0:T(256)}, u32[]{:S(2)}) copy-start(f32[256]{0:T(256)} %param.16) | copy-start | bytes 3076
  1.2 0.7 %copy-start.9 = (f32[256]{0:T(256)S(1)}, f32[256]{0:T(256)}, u32[]{:S(2)}) copy-start(f32[256]{0:T(256)} %param.17) | copy-start | bytes 3076
  1.2 0.7 %copy-start.10 = (f32[256]{0:T(256)S(1)}, f32[256]{0:T(256)}, u32[]{:S(2)}) copy-start(f32[256]{0:T(256)} %param.18) | copy-start | bytes 3076
  1.2 0.7 %copy-start.11 = (f32[256]{0:T(256)S(1)}, f32[256]{0:T(256)}, u32[]{:S(2)}) copy-start(f32[256]{0:T(256)} %param.22) | copy-start | bytes 3076
  1.3 0.7 %copy-start.12 = (f32[256]{0:T(256)S(1)}, f32[256]{0:T(256)}, u32[]{:S(2)}) copy-start(f32[256]{0:T(256)} %param.23) | copy-start | bytes 3076
  2.0 1.0 %copy-start = (bf16[32,32,256]{2,1,0:T(8,128)(2,1)S(1)}, bf16[32,32,256]{2,1,0:T(8,128)(2,1)}, u32[]{:S(2)}) copy-start(bf16[32,32,256]{2,1,0:T(8,128)(2,1)} %feat.1) | copy-start | bytes 1572868
  3.0 1.0 %copy-start.1 = (bf16[256,1024]{1,0:T(8,128)(2,1)S(1)}, bf16[256,1024]{1,0:T(8,128)(2,1)}, u32[]{:S(2)}) copy-start(bf16[256,1024]{1,0:T(8,128)(2,1)} %we_hbm.1) | copy-start | bytes 1572868
  4.1 1.0 %copy-start.2 = (bf16[1024,256]{1,0:T(8,128)(2,1)S(1)}, bf16[1024,256]{1,0:T(8,128)(2,1)}, u32[]{:S(2)}) copy-start(bf16[1024,256]{1,0:T(8,128)(2,1)} %wr_hbm.1) | copy-start | bytes 1572868
  5.1 0.9 %copy-start.4 = (bf16[256,256]{1,0:T(8,128)(2,1)S(1)}, bf16[256,256]{1,0:T(8,128)(2,1)}, u32[]{:S(2)}) copy-start(bf16[256,256]{1,0:T(8,128)(2,1)} %wq_hbm.1) | copy-start | bytes 393220
  6.0 0.9 %copy-start.5 = (bf16[256,256]{1,0:T(8,128)(2,1)S(1)}, bf16[256,256]{1,0:T(8,128)(2,1)}, u32[]{:S(2)}) copy-start(bf16[256,256]{1,0:T(8,128)(2,1)} %wo_hbm.1) | copy-start | bytes 393220

commit v2 on v1

--- a/solution.py
+++ b/solution.py
@@ -21,35 +21,52 @@
 
 
 def gelu(x):
-    return (0.5 * x) * (1.0 + lax.erf(x * 0.7071067811865476))
+    size = jnp.abs(x)
+    q = 1.0 + (0.3275911 * 0.7071067811865476) * size
+    t = pl.reciprocal(q, approx=True)
+    t = t * (2.0 - q * t)
+    p = 0.5 * 1.061405429 * t - 0.5 * 1.453152027
+    p = p * t + 0.5 * 1.421413741
+    p = p * t - 0.5 * 0.284496736
+    p = p * t + 0.5 * 0.254829592
+    tail = (p * t) * jnp.exp2((x * x) * (-0.5 * 1.4426950408889634))
+    return jnp.maximum(x, 0.0) - size * tail
 
 
 def kernel(
     n_row,
     n_col,
+    *refs,
+):
+    sources, out, local, rest = refs[:14], refs[14], refs[15:29], refs[29:]
+    body(n_row, n_col, sources, out, local, *local, *rest)
+
+
+def body(
+    n_row,
+    n_col,
+    sources,
+    out,
+    local,
     feat,
     dw,
     dw_bias,
     gain,
     nbias,
-    we_hbm,
+    we,
     b_exp,
-    wr_hbm,
+    wr,
     b_red,
     scale,
-    wq_hbm,
-    wkv_hbm,
-    table,
-    wo_hbm,
-    out,
-    we,
-    wr,
     wq,
     wkv,
+    rel,
     wo,
+    table,
     xs,
     taps,
     wb,
+    conv,
     norm,
     block,
     psum,
@@ -71,13 +88,10 @@
     stride = 2 * span
     keys = 4 * stride
 
-    weights = [
-        pltpu.make_async_copy(s, d, wsem.at[k])
-        for k, (s, d) in enumerate(
-            ((we_hbm, we), (wr_hbm, wr), (wq_hbm, wq), (wkv_hbm, wkv), (wo_hbm, wo))
-        )
+    loads = [
+        pltpu.make_async_copy(sources[k], local[k], wsem.at[k]) for k in range(len(local))
     ]
-    for c in weights:
+    for c in loads:
         c.start()
 
     up, down = row > 0, row < n_row - 1
@@ -123,6 +137,7 @@
             xs[h, pl.ds(base + L + T, 8)] = zero
         return carry
 
+    loads[0].wait()
     lax.fori_loop(0, T, widen, 0)
     for side, first in ((0, 0), (1, T - 3)):
         for c in range(3):
@@ -163,6 +178,8 @@
         def _(c=c):
             c.start()
 
+    for k in (1, 2, 3, 4, 6, 8, 9, 12):
+        loads[k].wait()
     for a in range(7):
         v = dw[a].astype(F32)
         for b in range(7):
@@ -172,7 +189,11 @@
                 )
     lane = lax.broadcasted_iota(jnp.int32, (8, keys), 1)
     valid = lax.rem(lane, stride) < span
+    table[...] = jnp.zeros(table.shape, F32)
     for r in range(4):
+        for k in range(4):
+            width = 2 * span - 1
+            table[r, :, k * stride : k * stride + width] = rel[k - r + 3]
         t = table[r]
         for c in range(4):
             shift = keys - (span - 1) + 4 * col + c
@@ -226,12 +247,11 @@
 
     lax.fori_loop(0, T + 6, spread_rows, 0)
 
-    weights[0].wait()
-    weights[1].wait()
+    loads[5].wait()
+    loads[7].wait()
 
     def region_row(i, carry):
         def column(j, carry):
-            x = []
             for h in range(2):
                 acc = jnp.broadcast_to(
                     dw_bias[:, h * 128 : h * 128 + 128].reshape(1, 1, 128), (8, 8, 128)
@@ -240,21 +260,20 @@
                     slab = taps[h, j + b, pl.ds(i * 8, 14)]
                     for a in range(7):
                         acc = acc + slab[a : a + 8] * wb[h, a * 7 + b]
-                x.append(acc.reshape(64, 128))
-            mean = (
-                jnp.sum(x[0] + x[1], axis=-1, keepdims=True) * (1.0 / 256.0)
-            )
+                conv[h, pl.ds(pl.multiple_of(j * 64, 64), 64)] = acc.reshape(64, 128)
+            return carry
+
+        lax.fori_loop(0, 4, column, 0)
+        for p in range(4):
+            at = slice(p * 64, p * 64 + 64)
+            x = [conv[h, at] for h in range(2)]
+            mean = jnp.sum(x[0] + x[1], axis=-1, keepdims=True) * (1.0 / 256.0)
             x = [v - mean for v in x]
             var = jnp.sum(x[0] * x[0] + x[1] * x[1], axis=-1, keepdims=True) * (1.0 / 256.0)
             inv = lax.rsqrt(var + 1e-06)
             for h in range(2):
                 lanes = slice(h * 128, h * 128 + 128)
-                norm[pl.ds(pl.multiple_of(j * 64, 64), 64), lanes] = (
-                    x[h] * inv * gain[:, lanes] + nbias[:, lanes]
-                ).astype(BF16)
-            return carry
-
-        lax.fori_loop(0, 4, column, 0)
+                norm[at, lanes] = (x[h] * inv * gain[:, lanes] + nbias[:, lanes]).astype(BF16)
         n = norm[...]
         red = jnp.zeros((256, 256), F32)
         for f in range(4):
@@ -295,9 +314,9 @@
         )
         c.start()
         gathers.append(c)
-    weights[2].wait()
-    weights[3].wait()
-    weights[4].wait()
+    loads[10].wait()
+    loads[11].wait()
+    loads[13].wait()
     queries = dot(pooled, wq[...]).astype(BF16).astype(F32)
     channel = lax.broadcasted_iota(jnp.int32, (8, 256), 1)
     head = lax.broadcasted_iota(jnp.int32, (8, 256), 0)
@@ -363,27 +382,27 @@
     rel_bias,
     w_out,
 ):
-    stride = 8 * n_col
-    keys = 4 * stride
-    padded = jnp.pad(rel_bias, ((0, 0), (0, 0), (0, 1)))
-    table = jnp.stack([padded[:, 3 - r : 7 - r].reshape(HEADS, keys) for r in range(4)])
+    lane = lambda v: v.reshape(1, -1)
+    keys = 32 * n_col
+    arrays = (
+        features, dw_kernel, lane(dw_bias), lane(norm_gain), lane(norm_bias), w_expand,
+        lane(b_expand), w_reduce, lane(b_reduce), lane(layer_scale), w_query, w_keyval,
+        jnp.transpose(rel_bias, (1, 0, 2)), w_out,
+    )
+    hbm = pl.BlockSpec(memory_space=pltpu.HBM)
     vmem = pl.BlockSpec(memory_space=pltpu.VMEM)
-    hbm = pl.BlockSpec(memory_space=pl.ANY)
-    lane = lambda v: v.reshape(1, -1)
     return pl.pallas_call(
         functools.partial(kernel, n_row, n_col),
         out_shape=jax.ShapeDtypeStruct(features.shape, BF16),
-        in_specs=[vmem] * 5 + [hbm, vmem, hbm, vmem, vmem, hbm, hbm, vmem, hbm],
+        in_specs=[hbm] * 14,
         out_specs=vmem,
-        scratch_shapes=[
-            pltpu.VMEM(w_expand.shape, BF16),
-            pltpu.VMEM(w_reduce.shape, BF16),
-            pltpu.VMEM(w_query.shape, BF16),
-            pltpu.VMEM(w_keyval.shape, BF16),
-            pltpu.VMEM(w_out.shape, BF16),
+        scratch_shapes=[pltpu.VMEM(v.shape, v.dtype) for v in arrays]
+        + [
+            pltpu.VMEM((4, 8, keys), F32),
             pltpu.VMEM((2, (T + 6) * W, 128), F32),
             pltpu.VMEM((2, 10, T + 6, 8, 128), F32),
             pltpu.VMEM((2, 49, 8, 128), F32),
+            pltpu.VMEM((2, 256, 128), F32),
             pltpu.VMEM((256, 256), BF16),
             pltpu.VMEM((2, T * T, 128), F32),
             pltpu.VMEM((2, 32, 128), F32),
@@ -393,31 +412,16 @@
             pltpu.VMEM((2, 3, T, 256), BF16),
             pltpu.VMEM((4, 3, 16, 256), BF16),
             pltpu.VMEM((n_col, 16, 256), BF16),
-            pltpu.SemaphoreType.DMA((5,)),
+            pltpu.SemaphoreType.DMA((14,)),
             pltpu.SemaphoreType.DMA((8,)),
             pltpu.SemaphoreType.DMA((8,)),
             pltpu.SemaphoreType.DMA((n_col - 1,)),
             pltpu.SemaphoreType.DMA((n_col - 1,)),
         ],
         compiler_params=pltpu.CompilerParams(
-            collective_id=0, has_side_effects=True, vmem_limit_bytes=40 * 1024 * 1024
+            collective_id=0, has_side_effects=True, vmem_limit_bytes=63 * 1024 * 1024
         ),
-    )(
-        features,
-        dw_kernel,
-        lane(dw_bias),
-        lane(norm_gain),
-        lane(norm_bias),
-        w_expand,
-        lane(b_expand),
-        w_reduce,
-        lane(b_reduce),
-        lane(layer_scale),
-        w_query,
-        w_keyval,
-        table,
-        w_out,
-    )
+    )(*arrays)
 
 
 def solution(mesh):

time: 31.7 us -> 25.8 us (0.81)
  local copies, waits for them, and re-layouts: 7.66 us -> 1.87 us
    unnamed x27 -> x1, local copies, waits for them, and re-layouts: 6.44 us -> 1.87 us
    slice x5 -> x0, local copies, waits for them, and re-layouts: 0.89 us -> none  [shards(): padded[:, 3 - r:7 - r].reshape(HEADS, keys)]
    another operation x4 -> x0, local copies, waits for them, and re-layouts: 0.33 us -> none  [shards(): jnp.stack([padded[:, 3 - r:7 - r].reshape(HEADS, keys) for r in range(4)])]
where the time goes in v2:
time: 25.8 us; the launch traced here: 25.6 us
  Pallas kernels  23.8 us (92%)
  local copies, waits for them, and re-layouts  1.87 us (7%)
    pallas_call x1, Pallas kernels, shards(): pl.pallas_call(functools.partial(kernel, n_row, n_col), out_shape=jax.Sha...  23.8 us
    unnamed x1, local copies, waits for them, and re-layouts  1.87 us

profile of v2, /device:TPU:17, one launch (start us, length us, event | category | flops | bytes accessed | tf_op | source)
XLA Modules:
  0.0 25.6 jit_solution(9818684010056793891)
XLA Ops:
  0.0 23.8 %shard_map.136 = bf16[32,32,256]{2,1,0:T(8,128)(2,1)} custom-call(bf16[32,32,256]{2,1,0:T(8,128)(2,1)} %refs_0_.1, bf16[7,7,256]{2,1,0:T(8,128)(2,1)} %refs_1_.1, f32[1,256]{1,0:T(1,128)} %bitcast.9, f32[1,256]{1,0:T(1,128)} %bitcast.10, f32[1,256]{1,0:T(1,128)} %bitcast.11, bf16[256,1024]{1,0:T(8,128)(2,1)} %refs_5_.1, f32[1,1024]{1,0:T(1,128)} %bitcast.8, ...), custom_call_target="tpu_custom_call" | custom-call | tf_op jit(solution)/shard_map/pallas_call | solution.py:394
  23.8 1.9 %copy.16 = bf16[32,32,256]{2,1,0:T(8,128)(2,1)} copy(bf16[32,32,256]{2,1,0:T(8,128)(2,1)} %shard_map.136) | data formatting | bytes 1048576

commit v3 on v2

--- a/solution.py
+++ b/solution.py
@@ -200,6 +200,39 @@
             moved = pltpu.roll(t, shift, 1)
             bias[r * 4 + c] = jnp.where(valid, moved, -1e30)
 
+    def split_row(r, columns):
+        for h in range(2):
+            for m in columns:
+                taps[h, m, r] = xs[h, pl.ds(r * W + (L - 3) + m, 8, stride=4)]
+
+    def own_columns(r, carry):
+        split_row(r, (3, 4, 5, 6))
+        return carry
+
+    lax.fori_loop(3, T + 3, own_columns, 0)
+
+    def add(acc, h, i, m, b):
+        slab = taps[h, m, pl.ds(i * 8, 14)]
+        for a in range(7):
+            acc = acc + slab[a : a + 8] * wb[h, a * 7 + b]
+        return acc
+
+    def inner(i, carry):
+        def column(j, carry):
+            for h in range(2):
+                acc = jnp.broadcast_to(
+                    dw_bias[:, h * 128 : h * 128 + 128].reshape(1, 1, 128), (8, 8, 128)
+                )
+                for m in range(3, 7):
+                    acc = add(acc, h, i, m, m - j)
+                conv[h, pl.ds((i * 4 + j) * 8, 8)] = acc
+            return carry
+
+        lax.fori_loop(0, 4, column, 0)
+        return carry
+
+    lax.fori_loop(1, 3, inner, 0)
+
     def halo(k):
         return sends[opposite[k]].wait_recv
 
@@ -239,13 +272,15 @@
                     for h in range(2):
                         xs[h, at : at + 1] = v[s : s + 1, h * 128 : h * 128 + 128]
 
-    def spread_rows(r, carry):
-        for h in range(2):
-            for m in range(10):
-                taps[h, m, r] = xs[h, pl.ds(r * W + (L - 3) + m, 8, stride=4)]
-        return carry
-
-    lax.fori_loop(0, T + 6, spread_rows, 0)
+    def others(r, carry):
+        split_row(r, (0, 1, 2, 7, 8, 9))
+        return carry
+
+    lax.fori_loop(3, T + 3, others, 0)
+    for r in (0, 1, 2, T + 3, T + 4, T + 5):
+        split_row(r, range(10))
+    inner(0, 0)
+    inner(3, 0)
 
     loads[5].wait()
     loads[7].wait()
@@ -253,20 +288,17 @@
     def region_row(i, carry):
         def column(j, carry):
             for h in range(2):
-                acc = jnp.broadcast_to(
-                    dw_bias[:, h * 128 : h * 128 + 128].reshape(1, 1, 128), (8, 8, 128)
-                )
-                for b in range(7):
-                    slab = taps[h, j + b, pl.ds(i * 8, 14)]
-                    for a in range(7):
-                        acc = acc + slab[a : a + 8] * wb[h, a * 7 + b]
-                conv[h, pl.ds(pl.multiple_of(j * 64, 64), 64)] = acc.reshape(64, 128)
+                acc = conv[h, pl.ds((i * 4 + j) * 8, 8)]
+                for k in range(3):
+                    b = k + 4 * lax.div(j + k, 3)
+                    acc = add(acc, h, i, j + b, b)
+                conv[h, pl.ds((i * 4 + j) * 8, 8)] = acc
             return carry
 
         lax.fori_loop(0, 4, column, 0)
         for p in range(4):
             at = slice(p * 64, p * 64 + 64)
-            x = [conv[h, at] for h in range(2)]
+            x = [conv[h, pl.ds(i * 32 + p * 8, 8)].reshape(64, 128) for h in range(2)]
             mean = jnp.sum(x[0] + x[1], axis=-1, keepdims=True) * (1.0 / 256.0)
             x = [v - mean for v in x]
             var = jnp.sum(x[0] * x[0] + x[1] * x[1], axis=-1, keepdims=True) * (1.0 / 256.0)
@@ -402,7 +434,7 @@
             pltpu.VMEM((2, (T + 6) * W, 128), F32),
             pltpu.VMEM((2, 10, T + 6, 8, 128), F32),
             pltpu.VMEM((2, 49, 8, 128), F32),
-            pltpu.VMEM((2, 256, 128), F32),
+            pltpu.VMEM((2, 128, 8, 128), F32),
             pltpu.VMEM((256, 256), BF16),
             pltpu.VMEM((2, T * T, 128), F32),
             pltpu.VMEM((2, 32, 128), F32),
@@ -419,9 +451,9 @@
             pltpu.SemaphoreType.DMA((n_col - 1,)),
         ],
         compiler_params=pltpu.CompilerParams(
-            collective_id=0, has_side_effects=True, vmem_limit_bytes=63 * 1024 * 1024
+            collective_id=0, has_side_effects=True, vmem_limit_bytes=40 * 1024 * 1024
         ),
-    )(*arrays)
+    )(*[pltpu.with_memory_space_constraint(v, pltpu.HBM) for v in arrays])
 
 
 def solution(mesh):

time: 25.8 us -> 22.2 us (0.86)
  Pallas kernels: 23.8 us -> 21.2 us
  local copies, waits for them, and re-layouts: 1.87 us -> 0.8 us
    pallas_call x1, Pallas kernels: 23.8 us -> 21.2 us  [shards(): pl.pallas_call(functools.partial(kernel, n_row, n_col), out_shape=jax.Sha...]
    unnamed x1, local copies, waits for them, and re-layouts: 1.87 us -> 0.8 us
where the time goes in v3:
time: 22.2 us; the launch traced here: 22 us
  Pallas kernels  21.2 us (95%)
  local copies, waits for them, and re-layouts  0.8 us (4%)
    pallas_call x1, Pallas kernels, shards(): pl.pallas_call(functools.partial(kernel, n_row, n_col), out_shape=jax.Sha...  21.2 us
    unnamed x1, local copies, waits for them, and re-layouts  0.8 us

profile of v3, /device:TPU:17, one launch (start us, length us, event | category | flops | bytes accessed | tf_op | source)
XLA Modules:
  0.0 22.0 jit_solution(5043648895188437569)
XLA Ops:
  0.0 21.2 %shard_map.136 = bf16[32,32,256]{2,1,0:T(8,128)(2,1)S(1)} custom-call(bf16[32,32,256]{2,1,0:T(8,128)(2,1)} %refs_0_.1, bf16[7,7,256]{2,1,0:T(8,128)(2,1)} %refs_1_.1, f32[1,256]{1,0:T(1,128)} %bitcast.9, f32[1,256]{1,0:T(1,128)} %bitcast.10, f32[1,256]{1,0:T(1,128)} %bitcast.11, bf16[256,1024]{1,0:T(8,128)(2,1)} %refs_5_.1, f32[1,1024]{1,0:T(1,128)} %bitcast.8, ...), custom_call_target="tpu_custom_call" | custom-call | tf_op jit(solution)/shard_map/pallas_call | solution.py:426
  21.3 0.8 %copy.16 = bf16[32,32,256]{2,1,0:T(8,128)(2,1)} copy(bf16[32,32,256]{2,1,0:T(8,128)(2,1)S(1)} %shard_map.136) | data formatting | bytes 1048576

commit v4 on v3

--- a/solution.py
+++ b/solution.py
@@ -138,7 +138,7 @@
         return carry
 
     loads[0].wait()
-    lax.fori_loop(0, T, widen, 0)
+    lax.fori_loop(0, T, widen, 0, unroll=4)
     for side, first in ((0, 0), (1, T - 3)):
         for c in range(3):
             for h in range(2):
@@ -209,7 +209,7 @@
         split_row(r, (3, 4, 5, 6))
         return carry
 
-    lax.fori_loop(3, T + 3, own_columns, 0)
+    lax.fori_loop(3, T + 3, own_columns, 0, unroll=4)
 
     def add(acc, h, i, m, b):
         slab = taps[h, m, pl.ds(i * 8, 14)]
@@ -276,7 +276,7 @@
         split_row(r, (0, 1, 2, 7, 8, 9))
         return carry
 
-    lax.fori_loop(3, T + 3, others, 0)
+    lax.fori_loop(3, T + 3, others, 0, unroll=4)
     for r in (0, 1, 2, T + 3, T + 4, T + 5):
         split_row(r, range(10))
     inner(0, 0)
@@ -393,7 +393,7 @@
         out[r] = jnp.concatenate(parts, axis=1).astype(BF16)
         return carry
 
-    lax.fori_loop(0, T, finish, 0)
+    lax.fori_loop(0, T, finish, 0, unroll=4)
 
 
 def shards(

time: 22.2 us -> 22 us (level)
  no operation moved by 1% of the time
where the time goes in v4:
time: 22 us; the launch traced here: 21.8 us
  Pallas kernels  21 us (95%)
  local copies, waits for them, and re-layouts  0.8 us (4%)
    pallas_call x1, Pallas kernels, shards(): pl.pallas_call(functools.partial(kernel, n_row, n_col), out_shape=jax.Sha...  21 us
    unnamed x1, local copies, waits for them, and re-layouts  0.8 us

profile of v4, /device:TPU:17, one launch (start us, length us, event | category | flops | bytes accessed | tf_op | source)
XLA Modules:
  0.0 21.8 jit_solution(16275958179807567634)
XLA Ops:
  0.0 21.0 %shard_map.136 = bf16[32,32,256]{2,1,0:T(8,128)(2,1)S(1)} custom-call(bf16[32,32,256]{2,1,0:T(8,128)(2,1)} %refs_0_.1, bf16[7,7,256]{2,1,0:T(8,128)(2,1)} %refs_1_.1, f32[1,256]{1,0:T(1,128)} %bitcast.9, f32[1,256]{1,0:T(1,128)} %bitcast.10, f32[1,256]{1,0:T(1,128)} %bitcast.11, bf16[256,1024]{1,0:T(8,128)(2,1)} %refs_5_.1, f32[1,1024]{1,0:T(1,128)} %bitcast.8, ...), custom_call_target="tpu_custom_call" | custom-call | tf_op jit(solution)/shard_map/pallas_call | solution.py:426
  21.0 0.8 %copy.16 = bf16[32,32,256]{2,1,0:T(8,128)(2,1)} copy(bf16[32,32,256]{2,1,0:T(8,128)(2,1)S(1)} %shard_map.136) | data formatting | bytes 1048576

commit v5 on v4

--- a/solution.py
+++ b/solution.py
@@ -228,7 +228,7 @@
                 conv[h, pl.ds((i * 4 + j) * 8, 8)] = acc
             return carry
 
-        lax.fori_loop(0, 4, column, 0)
+        lax.fori_loop(0, 4, column, 0, unroll=2)
         return carry
 
     lax.fori_loop(1, 3, inner, 0)
@@ -295,7 +295,7 @@
                 conv[h, pl.ds((i * 4 + j) * 8, 8)] = acc
             return carry
 
-        lax.fori_loop(0, 4, column, 0)
+        lax.fori_loop(0, 4, column, 0, unroll=4)
         for p in range(4):
             at = slice(p * 64, p * 64 + 64)
             x = [conv[h, pl.ds(i * 32 + p * 8, 8)].reshape(64, 128) for h in range(2)]

time: 22 us -> 21.3 us (0.968)
  Pallas kernels: 21 us -> 20.4 us
    pallas_call x1, Pallas kernels: 21 us -> 20.4 us  [shards(): pl.pallas_call(functools.partial(kernel, n_row, n_col), out_shape=jax.Sha...]
where the time goes in v5:
time: 21.3 us; the launch traced here: 21.2 us
  Pallas kernels  20.4 us (96%)
  local copies, waits for them, and re-layouts  0.8 us (4%)
    pallas_call x1, Pallas kernels, shards(): pl.pallas_call(functools.partial(kernel, n_row, n_col), out_shape=jax.Sha...  20.4 us
    unnamed x1, local copies, waits for them, and re-layouts  0.8 us

profile of v5, /device:TPU:17, one launch (start us, length us, event | category | flops | bytes accessed | tf_op | source)
XLA Modules:
  0.0 21.2 jit_solution(5315187249594387796)
XLA Ops:
  0.0 20.4 %shard_map.136 = bf16[32,32,256]{2,1,0:T(8,128)(2,1)S(1)} custom-call(bf16[32,32,256]{2,1,0:T(8,128)(2,1)} %refs_0_.1, bf16[7,7,256]{2,1,0:T(8,128)(2,1)} %refs_1_.1, f32[1,256]{1,0:T(1,128)} %bitcast.9, f32[1,256]{1,0:T(1,128)} %bitcast.10, f32[1,256]{1,0:T(1,128)} %bitcast.11, bf16[256,1024]{1,0:T(8,128)(2,1)} %refs_5_.1, f32[1,1024]{1,0:T(1,128)} %bitcast.8, ...), custom_call_target="tpu_custom_call" | custom-call | tf_op jit(solution)/shard_map/pallas_call | solution.py:426
  20.4 0.8 %copy.16 = bf16[32,32,256]{2,1,0:T(8,128)(2,1)} copy(bf16[32,32,256]{2,1,0:T(8,128)(2,1)S(1)} %shard_map.136) | data formatting | bytes 1048576

commit v6 on v5

--- a/solution.py
+++ b/solution.py
@@ -324,7 +324,7 @@
             psum[h, pl.ds(pl.multiple_of(i * 8, 8), 8)] = total
         return carry
 
-    lax.fori_loop(0, 4, region_row, 0)
+    lax.fori_loop(0, 4, region_row, 0, unroll=2)
 
     pooled = jnp.concatenate(
         [

time: 21.3 us -> 21.1 us (level)
  Pallas kernels: 20.4 us -> 20.1 us
    pallas_call x1, Pallas kernels: 20.4 us -> 20.1 us  [shards(): pl.pallas_call(functools.partial(kernel, n_row, n_col), out_shape=jax.Sha...]
where the time goes in v6:
time: 21.1 us; the launch traced here: 20.9 us
  Pallas kernels  20.1 us (95%)
  local copies, waits for them, and re-layouts  0.8 us (4%)
    pallas_call x1, Pallas kernels, shards(): pl.pallas_call(functools.partial(kernel, n_row, n_col), out_shape=jax.Sha...  20.1 us
    unnamed x1, local copies, waits for them, and re-layouts  0.8 us

profile of v6, /device:TPU:17, one launch (start us, length us, event | category | flops | bytes accessed | tf_op | source)
XLA Modules:
  0.0 20.9 jit_solution(12267097916971551037)
XLA Ops:
  0.0 20.1 %shard_map.136 = bf16[32,32,256]{2,1,0:T(8,128)(2,1)S(1)} custom-call(bf16[32,32,256]{2,1,0:T(8,128)(2,1)} %refs_0_.1, bf16[7,7,256]{2,1,0:T(8,128)(2,1)} %refs_1_.1, f32[1,256]{1,0:T(1,128)} %bitcast.9, f32[1,256]{1,0:T(1,128)} %bitcast.10, f32[1,256]{1,0:T(1,128)} %bitcast.11, bf16[256,1024]{1,0:T(8,128)(2,1)} %refs_5_.1, f32[1,1024]{1,0:T(1,128)} %bitcast.8, ...), custom_call_target="tpu_custom_call" | custom-call | tf_op jit(solution)/shard_map/pallas_call | solution.py:426
  20.1 0.8 %copy.16 = bf16[32,32,256]{2,1,0:T(8,128)(2,1)} copy(bf16[32,32,256]{2,1,0:T(8,128)(2,1)S(1)} %shard_map.136) | data formatting | bytes 1048576
